TPU v7x, 32 devices: a whole 2x2x4 slice. The times are simulated.
32 devices in a mesh: az: 16 (over z, x, core), rad: 2 (over y).
Axes of the slice: x: 2, y: 2, z: 4, core: 2. Of those that a mesh axis runs over, the one named last changes fastest.
Arguments:
- pressure: float32 [2, 256, 192, 128], P(None, 'az', 'rad'), may hold values from -6 to 6
- source: float32 [2, 256, 192, 128], P(None, 'az', 'rad'), may hold values from -6 to 6
- diagonal: float32 [2, 256, 192, 128], P(None, 'az', 'rad'), may hold values from 0.5 to 8
- rot_offset: int32 [1], replicated, may hold values from 0 to 255
Outputs:
- corrected: float32 [2, 256, 192, 128], P(None, 'az', 'rad')
All inputs are finite; a program needn't handle non-finite values.
Results may differ from a plain program's by a relative error of at most 0.00002.
Values sent between devices are 32-bit elements; how exact they have to be, the bound alone decides.
No kernel may reach another device: no remote copies, remote signals or barrier semaphores. Data moves between devices by JAX's collectives and lax.ppermute only.
A program may use at most 64 MiB of HBM per device.

v0:
```python
import functools

import jax
import jax.numpy as jnp
from jax import lax
from jax.experimental import pallas as pl
from jax.experimental.pallas import tpu as pltpu
from jax.sharding import PartitionSpec as P

STEPS = 2
SWEEPS = 4
OMEGA = 0.8
TILE = 8
OWN = 2 * TILE
LEVELS = tuple(range(SWEEPS))
WEIGHTS = (SWEEPS, SWEEPS + 1)


class Side:
    def __init__(self, low, radial_cells):
        end = OWN + radial_cells
        self.low = low
        self.own = slice(OWN, end)
        self.first = OWN if low else TILE
        self.count = radial_cells + TILE
        self.rows = slice(self.first, self.first + self.count)
        self.cut = slice(end, end + SWEEPS) if low else slice(OWN - SWEEPS, OWN)
        self.tile = slice(end, end + TILE) if low else slice(TILE, OWN)
        self.ghost = OWN - 1 if low else end
        self.edge = OWN if low else end - 1
        self.spare = self.count - 1 if low else 0
        self.inside = shifted(self.own, -self.first)
        self.facing = 1 if low else 0
        self.sent = slice(radial_cells - SWEEPS, radial_cells) if low else slice(0, SWEEPS)
        self.sent_tile = radial_cells - TILE if low else 0
        self.edge_tile = 0 if low else radial_cells - TILE

    def beyond(self, distance):
        return self.inside.stop - 1 + distance if self.low else self.inside.start - distance


def shifted(s, by):
    return slice(s.start + by, s.stop + by)


def axial_sum(x):
    lane = lax.broadcasted_iota(jnp.int32, x.shape, 1)
    last = x.shape[1] - 1
    return jnp.where(lane == 0, 0.0, pltpu.roll(x, 1, 1)) + jnp.where(
        lane == last, 0.0, pltpu.roll(x, last, 1)
    )


def neighbour_matrix(lanes):
    gap = lax.broadcasted_iota(jnp.int32, (lanes, lanes), 0) - lax.broadcasted_iota(
        jnp.int32, (lanes, lanes), 1
    )
    return jnp.where(jnp.abs(gap) == 1, 1.0, 0.0).astype(jnp.bfloat16)


def axial_product(x, matrix):
    high = x.astype(jnp.bfloat16)
    low = (x - high.astype(jnp.float32)).astype(jnp.bfloat16)
    return jnp.dot(high, matrix, preferred_element_type=jnp.float32) + jnp.dot(
        low, matrix, preferred_element_type=jnp.float32
    )


def relax_all(side, matrix, items, share=1 / 2):
    by_matrix = int(len(items) * share) // 2 * 2
    axial = []
    if by_matrix:
        here = jnp.concatenate([item[0][side.rows] for item in items[:by_matrix]], axis=0)
        product = axial_product(here, matrix)
        axial = [product[i * side.count : (i + 1) * side.count] for i in range(by_matrix)]
    for i, (column, beside, weight, shift, take) in enumerate(items):
        here = column[side.rows]
        radial = column[shifted(side.rows, -1)] + column[shifted(side.rows, 1)]
        nbr = beside() + radial + (axial[i] if i < by_matrix else axial_sum(here))
        kept = (1.0 - OMEGA) * here
        if shift is not None:
            kept = kept + shift()
        take(kept + weight() * nbr)


def on_each_side(radial_cells, body):
    low = lax.axis_index("rad") == 0

    @pl.when(low)
    def _():
        body(Side(True, radial_cells))

    @pl.when(jnp.logical_not(low))
    def _():
        body(Side(False, radial_cells))


def copy_all(copies):
    for c in copies:
        c.start()
    for c in copies:
        c.wait()


def end_columns(edge, cells, count):
    return slice(0, count) if edge == 0 else slice(cells - count, cells)


def block_rows(cells):
    return cells // 2 + SWEEPS - 1


class Message:
    def __init__(self, slots, radial_cells, cells, weights):
        self.slots = slots
        self.radial_cells = radial_cells
        tail = []
        needed = [(n, SWEEPS - 1 - n) for n in LEVELS] + [(SWEEPS, 2)] * weights
        tail += [(slot, k, h) for slot, n in needed for k in range(2) for h in range(1, n + 1)]
        tail += [("block", i) for i in range(block_rows(cells))]
        tail += ["third"] * weights
        start = 2 * len(slots) * radial_cells
        self.tail = {what: start + i for i, what in enumerate(tail)}
        self.rows = start + -(-len(tail) // TILE) * TILE

    def block(self, slot, k):
        start = (2 * self.slots.index(slot) + k) * self.radial_cells
        return slice(start, start + self.radial_cells)

    def row(self, *what):
        at = self.tail[what if len(what) > 1 else what[0]]
        return slice(at, at + 1)

    def beyond(self, slot, k):
        return [w[2] for w in self.tail if w != "third" and w[:2] == (slot, k) and len(w) == 3]

    def put(self, ref, side, slot, k, value):
        ref[self.block(slot, k)] = value[side.inside]
        for h in self.beyond(slot, k):
            at = side.beyond(h)
            ref[self.row(slot, k, h)] = value[at : at + 1]


def message_of(step, radial_cells, cells):
    return Message(LEVELS + WEIGHTS if step == 1 else LEVELS, radial_cells, cells, step == 1)


def close(column, side, facing):
    row = slice(side.ghost, side.ghost + 1)
    if facing:
        column[row] = jnp.zeros((1, column.shape[1]), jnp.float32)
    else:
        column[row] = column[side.edge : side.edge + 1]


def trajectories(side, field, other, weight, shift, layout, messages, weights):
    bufs = (field, other)
    matrix = neighbour_matrix(field.shape[-1])

    def at(edge, distance, n):
        return distance - 1 if edge == 0 else n - distance

    for edge in range(2):
        for k in range(2):
            for i in range(SWEEPS):
                close(field.at[edge, k, i], side, k == side.facing)
    for sweep in range(SWEEPS):
        src, dst = bufs[sweep % 2], bufs[1 - sweep % 2]
        items = []
        for edge, message in enumerate(messages):
            for k in range(2):
                layout.put(
                    message, side, sweep, k, src[edge, k, at(edge, 1, SWEEPS), side.rows]
                )
                for j in range(1, SWEEPS - sweep):
                    i = at(edge, j, SWEEPS - 1)

                    def beside(edge=edge, k=k, j=j):
                        total = src[edge, k, at(edge, j + 1, SWEEPS), side.rows]
                        if j > 1:
                            total = total + src[edge, k, at(edge, j - 1, SWEEPS), side.rows]
                        return total

                    def take(new, edge=edge, k=k, j=j):
                        out = dst.at[edge, k, at(edge, j, SWEEPS)]
                        out[side.rows] = new
                        close(out, side, k == side.facing)

                    items.append(
                        (
                            src.at[edge, k, at(edge, j, SWEEPS)],
                            beside,
                            functools.partial(weight, edge, k, i),
                            functools.partial(shift, edge, k, i),
                            take,
                        )
                    )
        relax_all(side, matrix, items, 3 / 4)
    if not weights:
        return
    for edge, message in enumerate(messages):
        for k in range(2):
            for i in range(2):
                layout.put(
                    message, side, SWEEPS + i, k, weight(edge, k, at(edge, 1 + i, SWEEPS - 1))
                )
        row = side.edge - side.first
        message[layout.row("third")] = weight(edge, side.facing, at(edge, 3, SWEEPS - 1))[
            row : row + 1
        ]


def pack(p_ref, s_ref, d_ref, cut_ref, edge_ref, p_ends, s_ends, d_ends, *rest):
    tiles, edge_tiles, sems = rest
    cells, radial_cells = p_ref.shape[1:3]

    def body(side):
        copies = []

        def fetch(source, target):
            copies.append(pltpu.make_async_copy(source, target, sems.at[len(copies)]))

        rows = pl.ds(side.sent_tile, TILE)
        for i, x in enumerate((p_ref, s_ref, d_ref)):
            fetch(x.at[:, :, rows, :], tiles.at[i])
        fetch(p_ref.at[side.facing, :, pl.ds(side.edge_tile, TILE), :], edge_tiles)
        for source, target in ((p_ref, p_ends), (s_ref, s_ends), (d_ref, d_ends)):
            count = target.shape[2]
            for edge in range(2):
                span = pl.ds(end_columns(edge, cells, count).start, count)
                fetch(source.at[:, span], target.at[edge])
        for c in copies:
            c.start()
        for c in copies[:4]:
            c.wait()
        cut_ref[...] = tiles[:, :, :, shifted(side.sent, -side.sent_tile), :]
        at = side.edge - OWN - side.edge_tile
        for j in range(cells):
            edge_ref[j : j + 1] = edge_tiles[j, at : at + 1]
        for c in copies[4:]:
            c.wait()

    on_each_side(radial_cells, body)


def fill_ends(field, side, p_ends, cut_ref, cells):
    for edge in range(2):
        columns = end_columns(edge, cells, SWEEPS)
        for k in range(2):
            for i in range(SWEEPS):
                field[edge, k, i, side.own] = p_ends[edge, k, i]
                field[edge, k, i, side.cut] = cut_ref[0, k, columns.start + i]


def send_block(layout, arriving, block, messages):
    arriving.wait()
    cells = block.shape[0]
    count = block_rows(cells)
    for edge, message in enumerate(messages):
        for i in range(count):
            at = i if edge == 0 else cells - count + i
            message[layout.row("block", i)] = block[at : at + 1]


def first_edges(
    p_ends, s_ends, d_ends, cut_ref, block_ref, last, first, block, sem, field, other, weight, shift
):
    radial_cells = p_ends.shape[3]
    cells = cut_ref.shape[2]
    n = SWEEPS - 1
    layout = message_of(1, radial_cells, cells)

    def body(side):
        arriving = pltpu.make_async_copy(block_ref, block, sem)
        arriving.start()
        own = shifted(side.own, -side.first)
        cut = shifted(side.cut, -side.first)
        fill_ends(field, side, p_ends, cut_ref, cells)
        for edge in range(2):
            columns = end_columns(edge, cells, n)
            for k in range(2):
                for i in range(n):
                    for rows, s, d in (
                        (own, s_ends[edge, k, i], d_ends[edge, k, i]),
                        (cut, cut_ref[1, k, columns.start + i], cut_ref[2, k, columns.start + i]),
                    ):
                        w = OMEGA / (6.0 + d)
                        weight[edge, k, i, rows] = w
                        shift[edge, k, i, rows] = w * s
        trajectories(
            side,
            field,
            other,
            lambda e, k, i: weight[e, k, i],
            lambda e, k, i: shift[e, k, i],
            layout,
            (first, last),
            True,
        )
        send_block(layout, arriving, block, (first, last))

    on_each_side(radial_cells, body)


def later_edges(p_ends, b_ends, w_ends, cut_ref, block_ref, last, first, block, sem, field, other):
    cells, radial_cells = cut_ref.shape[2], p_ends.shape[3]
    layout = message_of(2, radial_cells, cells)

    def body(side):
        arriving = pltpu.make_async_copy(block_ref, block, sem)
        arriving.start()
        fill_ends(field, side, p_ends, cut_ref, cells)
        trajectories(
            side,
            field,
            other,
            lambda e, k, i: w_ends[e, k, i + e],
            lambda e, k, i: b_ends[e, k, i + e],
            layout,
            (first, last),
            False,
        )
        send_block(layout, arriving, block, (first, last))

    on_each_side(radial_cells, body)


def inner_sweeps(side, levels, weight, shift, last, stash, tile_out, w_tile):
    cells = levels.shape[2]
    radial_cells = side.own.stop - side.own.start
    for j in range(cells):
        for k in range(2):
            close(levels.at[0, k, j], side, k == side.facing)
        for n in range(1, SWEEPS):
            close(levels.at[n, side.facing, j], side, True)
    at = side.edge - side.first
    for e, first in enumerate((0, cells - 2)):
        for k in range(2):
            for i in range(2):
                stash[e, 0, k, i] = levels[0, k, first + i]
    matrix = neighbour_matrix(levels.shape[-1])
    for n in range(SWEEPS):
        final = n == SWEEPS - 1

        def step(i, carry, n=n, final=final):
            items = []
            for k in (1, 0):
                for j in (n + 1 + 2 * i, n + 2 + 2 * i):

                    def beside(k=k, j=j):
                        return levels[n, k, j - 1, side.rows] + levels[n, k, j + 1, side.rows]

                    def take(new, k=k, j=j):
                        if final:
                            last[k, j - SWEEPS] = new[shifted(side.own, -side.first)]
                            return
                        levels[n + 1, k, j, side.rows] = new
                        if k != side.facing:
                            levels[n + 1, k, j, side.ghost : side.ghost + 1] = new[at : at + 1]

                    items.append(
                        (
                            levels.at[n, k, j],
                            beside,
                            functools.partial(lambda k, j: weight[k, j], k, j),
                            functools.partial(lambda k, j: shift[k, j], k, j),
                            take,
                        )
                    )
            relax_all(side, matrix, items)
            return carry

        lax.fori_loop(0, cells // 2 - 1 - n, step, 0, unroll=2 if n % 2 else 1)
        if not final:
            for e, first in enumerate((n + 1, cells - 3 - n)):
                for k in range(2):
                    for i in range(2):
                        stash[e, n + 1, k, i] = levels[n + 1, k, first + i]
    tile_out[...] = last[side.facing, :, side.edge_tile : side.edge_tile + TILE, :]
    first = side.edge_tile + OWN - side.first
    w_tile[...] = weight[side.facing, :, first : first + TILE, :]


def first_interior(
    p_ref, s_ref, d_ref, cut_ref,
    stash, tile_out, w_tile, cut_out, b_ends, w_ends, inner_out, b_out, w_out,
    levels, last, shift, weight, sems,
):
    cells, radial_cells = p_ref.shape[1:3]

    def body(side):
        own = pl.ds(OWN - side.first, radial_cells)
        copy_all(
            [
                pltpu.make_async_copy(
                    p_ref, levels.at[0, :, :, pl.ds(OWN, radial_cells), :], sems.at[0]
                ),
                pltpu.make_async_copy(s_ref, shift.at[:, :, own, :], sems.at[1]),
                pltpu.make_async_copy(d_ref, weight.at[:, :, own, :], sems.at[2]),
            ]
        )
        cut = shifted(side.cut, -side.first)
        levels[0, :, :, side.cut, :] = cut_ref[0]
        shift[:, :, cut, :] = cut_ref[1]
        weight[:, :, cut, :] = cut_ref[2]

        def invert(j, carry):
            for k in range(2):
                w = OMEGA / (6.0 + weight[k, j])
                weight[k, j] = w
                shift[k, j] = w * shift[k, j]
            return carry

        lax.fori_loop(0, cells, invert, 0)
        pending = [
            pltpu.make_async_copy(shift, b_out, sems.at[1]),
            pltpu.make_async_copy(weight, w_out, sems.at[2]),
        ]
        for c in pending:
            c.start()
        for e in range(2):
            columns = end_columns(e, cells, SWEEPS)
            b_ends[e] = shift[:, columns]
            w_ends[e] = weight[:, columns]
        inner_sweeps(side, levels, weight, shift, last, stash, tile_out, w_tile)
        pending.append(pltpu.make_async_copy(last, inner_out, sems.at[0]))
        pending[-1].start()
        cut_out[...] = last[:, :, side.sent, :]
        for c in pending:
            c.wait()

    on_each_side(radial_cells, body)


def later_interior(
    inner_ref, tile_ref, p_ends, b_ref, w_ref, cut_ref,
    out_ref, stash, tile_out, w_tile,
    levels, last, shift, weight, sems,
):
    cells, radial_cells = out_ref.shape[1:3]
    inner = slice(SWEEPS, cells - SWEEPS)

    def body(side):
        copies = [
            pltpu.make_async_copy(b_ref, shift, sems.at[0]),
            pltpu.make_async_copy(w_ref, weight, sems.at[1]),
            pltpu.make_async_copy(
                inner_ref,
                levels.at[
                    0, :, pl.ds(SWEEPS, cells - 2 * SWEEPS), pl.ds(OWN, radial_cells), :
                ],
                sems.at[2],
            ),
        ]
        for c in copies:
            c.start()
        start = OWN + side.edge_tile
        for e in range(2):
            levels[0, :, end_columns(e, cells, SWEEPS), side.own, :] = p_ends[e]
        levels[0, :, :, side.cut, :] = cut_ref[0]
        for c in copies:
            c.wait()
        levels[0, side.facing, inner, start : start + TILE, :] = tile_ref[...]
        inner_sweeps(side, levels, weight, shift, last, stash, tile_out, w_tile)
        copy_all([pltpu.make_async_copy(last, out_ref.at[:, pl.ds(SWEEPS, cells - 2 * SWEEPS)], sems.at[0])])

    on_each_side(radial_cells, body)


def ghost_response(side, step, turn_ref, w_tile, block_ref, layout, messages, weights, wide, source):
    facing = side.facing
    cells = w_tile.shape[0]
    reach = SWEEPS - 1
    tile = slice(side.edge_tile + OWN - side.first, side.edge_tile + OWN - side.first + TILE)
    at = side.edge - OWN - side.edge_tile
    count = block_rows(cells)
    for i in range(count):
        for message, to in zip(messages, (cells - count + i, 2 * cells + i)):
            wide[to : to + 1] = message[layout.row("block", i)]
    wide[cells : 2 * cells] = block_ref[...]
    source[...] = jnp.zeros(source.shape, jnp.float32)
    offset = lax.rem(turn_ref[0] * step, cells * lax.axis_size("az"))
    rest = offset - lax.div(offset + cells // 2, cells) * cells
    start = cells - reach + (-rest if side.low else rest)
    for c in range(cells + 2 * reach):
        source[c, at : at + 1] = wide[pl.ds(start + c, 1), :]
    row = lax.broadcasted_iota(jnp.int32, source.shape[1:], 0)
    weight = [w_tile[j] for j in range(cells)]
    for e in range(2):
        far = weights[e][facing, 1, side.spare : side.spare + 1]
        beyond = [
            weights[e][facing, 0, tile],
            weights[e][facing, 1, tile],
            jnp.where(row == at, far, 0.0),
        ]
        weight = beyond[::-1] + weight if e == 0 else weight + beyond
    given = [source[c] for c in range(cells + 2 * reach)]
    response = [w * g for w, g in zip(weight, given)]
    for n in range(1, SWEEPS):
        old = response
        response = list(old)
        for c in range(n, len(old) - n):
            x = old[c]
            radial = jnp.where(row == 0, 0.0, pltpu.roll(x, 1, 0)) + jnp.where(
                row == TILE - 1, 0.0, pltpu.roll(x, TILE - 1, 0)
            )
            nbr = (old[c - 1] + old[c + 1]) + (radial + axial_sum(x)) + given[c]
            response[c] = (1.0 - OMEGA) * x + weight[c] * nbr
    return response[reach : reach + cells]


def finish(step, turn_ref, b_ends, w_ends, w_tile, stash, block_ref, tile_in, left_ref, right_ref, *rest):
    known = step > 1
    if known:
        beyond, _, out_ref, levels, last, inner_tiles, near, near2, wide, source, sems = rest
    else:
        cut_in, cut_out, edge_out, last, inner_tiles, beyond, *rest = rest
        levels, near, near2, wide, source = rest
    weights = (beyond.at[0], beyond.at[1])
    messages = (left_ref, right_ref)
    cells, radial_cells = block_ref.shape[0], last.shape[3]
    layout = message_of(step, radial_cells, cells)

    def given(e, k, slot):
        return messages[e][layout.block(slot, k)]

    def column(e, d):
        return d - 1 if e == 0 else cells - d

    def body(side):
        facing = side.facing

        def at(n, e, k, d):
            if d <= n:
                return levels.at[n, e, k, d]
            return stash.at[e, n, k, d - n - 1 if e == 0 else n + 2 - d]

        def meet(e, k, n, response):
            target = levels.at[n, e, k, 0]
            value = given(e, k, n)
            target[side.own] = value if response is None else value + response[side.inside]
            for h in layout.beyond(n, k):
                at = side.beyond(h)
                value = messages[e][layout.row(n, k, h)]
                if response is not None:
                    value = value + response[at : at + 1]
                target[side.first + at : side.first + at + 1] = value

        for e in range(2):
            if not known:
                for k in range(2):
                    for i in range(2):
                        target = beyond.at[e, k, i]
                        target[side.inside] = given(e, k, SWEEPS + i)
                        for h in layout.beyond(SWEEPS + i, k):
                            row = side.beyond(h)
                            target[row : row + 1] = messages[e][layout.row(SWEEPS + i, k, h)]
                beyond[e, facing, 1, side.spare : side.spare + 1] = messages[e][
                    layout.row("third")
                ]
            for k in range(2):
                meet(e, k, 0, None)
                for buf in (near, near2):
                    buf[e, k] = jnp.zeros(buf.shape[2:], jnp.float32)
        nears = (near, near2)

        matrix = neighbour_matrix(levels.shape[-1])

        def own_column(n, e, k, d, take):
            i = d - 1 if e == 0 else SWEEPS - d
            return (
                at(n, e, k, d),
                lambda: at(n, e, k, d - 1)[side.rows] + at(n, e, k, d + 1)[side.rows],
                lambda: w_ends[e, k, i],
                lambda: b_ends[e, k, i],
                take,
            )

        for n in range(SWEEPS - 1):
            src, dst = nears[n % 2], nears[1 - n % 2]
            items = []
            for e in range(2):
                for k in range(2):
                    for d in range(1, n + 2):

                        def take(new, e=e, k=k, d=d):
                            levels[n + 1, e, k, d, side.rows] = new
                            close(levels.at[n + 1, e, k, d], side, k == facing)

                        items.append(own_column(n, e, k, d, take))

                    def take(new, e=e, k=k):
                        dst[e, k, 0, side.rows] = new
                        meet(e, k, n + 1, new)
                        close(dst.at[e, k, 0], side, k == facing)

                    if n == 0:
                        take(weights[e][k, 0] * at(n, e, k, 1)[side.rows])
                        continue
                    items.append(
                        (
                            src.at[e, k, 0],
                            lambda e=e, k=k: at(n, e, k, 1)[side.rows] + src[e, k, 1, side.rows],
                            lambda e=e, k=k: weights[e][k, 0],
                            None,
                            take,
                        )
                    )
                    if n == 1:
                        dst[e, k, 1, side.rows] = weights[e][k, 1] * src[e, k, 0, side.rows]
            relax_all(side, matrix, items)
        copies = []

        def store(source, k, columns, rows):
            if known:
                target = out_ref.at[k, pl.ds(*columns), pl.ds(*rows), :]
                copies.append(pltpu.make_async_copy(source, target, sems.at[len(copies)]))
                copies[-1].start()

        response = None
        tile = slice(side.edge_tile, side.edge_tile + TILE)
        for k in (1 - facing, facing):
            if k == facing:
                response = ghost_response(
                    side, step, turn_ref, w_tile, block_ref, layout, messages, weights, wide, source
                )
                for i in range(cells - 2 * SWEEPS):
                    inner_tiles[i] = tile_in[i] + response[SWEEPS + i]
                columns = (SWEEPS, cells - 2 * SWEEPS)
                store(inner_tiles, k, columns, (side.edge_tile, TILE))
            items = []
            for d in range(1, SWEEPS + 1):
                for e in range(2):
                    first = end_columns(e, cells, SWEEPS).start

                    def take(new, e=e, k=k, i=column(e, d) - first, first=first):
                        new = new[shifted(side.own, -side.first)]
                        last[e, k, i] = new
                        if k == facing:
                            last[e, k, i, tile] = new[tile] + response[first + i]

                    items.append(own_column(SWEEPS - 1, e, k, d, take))
            relax_all(side, matrix, items)
            for e in range(2):
                first = end_columns(e, cells, SWEEPS).start
                store(last.at[e, k], k, (first, SWEEPS), (0, radial_cells))
        if not known:
            row = side.edge - OWN
            cut_out[0, :, SWEEPS : cells - SWEEPS] = cut_in[...]
            for i in range(cells - 2 * SWEEPS):
                j = SWEEPS + i
                r = row - side.edge_tile
                edge_out[j : j + 1] = inner_tiles[i, r : r + 1]
            for e in range(2):
                first = end_columns(e, cells, SWEEPS).start
                cut_out[0, :, first : first + SWEEPS] = last[e, :, :, side.sent, :]
                for i in range(SWEEPS):
                    edge_out[first + i : first + i + 1] = last[e, facing, i, row : row + 1]
        for c in copies:
            c.wait()

    on_each_side(radial_cells, body)


def ring(size, step):
    return [(i, (i + step) % size) for i in range(size)]


def facing_pairs(size, turn):
    pairs = []
    for i in range(size):
        pairs.append((2 * ((i - turn) % size) + 1, 2 * i))
        pairs.append((2 * ((i + turn) % size), 2 * i + 1))
    return pairs


def far_pairs(size, turn):
    return [(2 * i + r, 2 * ((i + (2 * r - 1) * turn) % size) + r) for i in range(size) for r in range(2)]


def facing_block(edge, offset):
    size = lax.axis_size("az")
    cells = edge.shape[0]
    turn = (offset + cells // 2) // cells % size
    near = min(size, 16)

    def far(t):
        return lambda e: lax.ppermute(e, ("az", "rad"), far_pairs(size, t * near))

    def branch(t):
        return lambda e: lax.ppermute(e, ("az", "rad"), facing_pairs(size, t))

    if size > near:
        edge = lax.switch(turn // near, [far(t) for t in range(-(-size // near))], edge)
    return lax.switch(turn % near, [branch(t) for t in range(near)], edge)


def per_device(pressure, source, diagonal, rot_offset):
    _, cells, radial_cells, lanes = pressure.shape
    size = lax.axis_size("az")
    rows, span = radial_cells + 4 * TILE, radial_cells + TILE

    def array(*shape):
        return jax.ShapeDtypeStruct(shape, jnp.float32)

    def scratch(*shape):
        return pltpu.VMEM(shape, jnp.float32)

    def pinned(x):
        return pltpu.with_memory_space_constraint(x, pltpu.HBM)

    kept = pltpu.HBM((2, cells, span, lanes), jnp.float32)
    kept_ends = array(2, 2, SWEEPS, span, lanes)
    stash = array(2, SWEEPS, 2, 2, rows, lanes)
    cells_in = cells - 2 * SWEEPS
    tiles = array(cells_in, TILE, lanes)
    vmem = pl.BlockSpec(memory_space=pltpu.VMEM)
    smem = pl.BlockSpec(memory_space=pltpu.SMEM)
    hbm = pl.BlockSpec(memory_space=pltpu.HBM)
    anywhere = pl.BlockSpec(memory_space=pl.ANY)
    columns = scratch(2, 2, SWEEPS, rows, lanes)
    three = scratch(2, 2, SWEEPS - 1, span, lanes)

    def call(kernel, out_shape, in_specs, out_specs, scratch_shapes, operands, work_columns, **more):
        work = 2 * work_columns * span * lanes
        return pl.pallas_call(
            kernel,
            out_shape=out_shape,
            in_specs=in_specs,
            out_specs=out_specs,
            scratch_shapes=scratch_shapes,
            compiler_params=pltpu.CompilerParams(vmem_limit_bytes=28 << 20),
            cost_estimate=pl.CostEstimate(
                flops=12 * work, bytes_accessed=8 * work, transcendentals=0
            ),
            **more,
        )(*operands)

    fields = tuple(pinned(x) for x in (pressure, source, diagonal))
    cut, edge, *ends = call(
        pack,
        (
            array(3, 2, cells, SWEEPS, lanes),
            array(cells, lanes),
            array(2, 2, SWEEPS, radial_cells, lanes),
            array(2, 2, SWEEPS - 1, radial_cells, lanes),
            array(2, 2, SWEEPS - 1, radial_cells, lanes),
        ),
        [hbm] * 3,
        [vmem] * 5,
        [
            scratch(3, 2, cells, TILE, lanes),
            scratch(cells, TILE, lanes),
            pltpu.SemaphoreType.DMA((10,)),
        ],
        fields,
        1,
        name="pack",
    )
    for step in range(1, STEPS + 1):
        known = step > 1
        cut = lax.ppermute(cut, "rad", [(0, 1), (1, 0)])
        offset = rot_offset[0] * step % (cells * size)
        block = facing_block(edge, offset)
        message = array(message_of(step, radial_cells, cells).rows, lanes)
        last, first = call(
            later_edges if known else first_edges,
            (message, message),
            [vmem] * 4 + [anywhere],
            [vmem] * 2,
            [scratch(cells, lanes), pltpu.SemaphoreType.DMA, columns, columns]
            + ([] if known else [three] * 2),
            (*ends, cut, block),
            12,
            name="edges",
        )
        left = lax.ppermute(last, "az", ring(size, 1))
        right = lax.ppermute(first, "az", ring(size, -1))
        result = pltpu.HBM(pressure.shape, jnp.float32)
        inner_shape = (2, cells_in, radial_cells, lanes)
        outs = (stash, tiles, array(cells, TILE, lanes))
        levels = scratch(SWEEPS, 2, cells, rows, lanes)
        whole = [scratch(*kept.shape), scratch(*kept.shape), pltpu.SemaphoreType.DMA((3,))]
        if not known:
            saved, inner_tiles, w_tile, inner_cut, b_ends, w_ends, inner, shift, weight = call(
                first_interior,
                (
                    *outs,
                    array(2, cells_in, SWEEPS, lanes),
                    *[kept_ends] * 2,
                    pltpu.HBM(inner_shape, jnp.float32),
                    *[kept] * 2,
                ),
                [hbm] * 3 + [vmem],
                [vmem] * 6 + [hbm] * 3,
                [levels, scratch(*inner_shape), *whole],
                (*fields, cut),
                44,
                name="interior",
            )
        else:
            done, saved, inner_tiles, w_tile = call(
                later_interior,
                (result, *outs),
                [hbm] + [vmem] * 2 + [hbm] * 2 + [vmem],
                [hbm] + [vmem] * 3,
                [levels, scratch(*inner_shape), *whole],
                (pinned(inner), fixed_tiles, ends[0], pinned(shift), pinned(weight), cut),
                44,
                name="interior",
            )
        operands = (
            rot_offset,
            b_ends,
            w_ends,
            w_tile,
            saved,
            block,
            inner_tiles,
            left,
            right,
        )
        last = (2, 2, SWEEPS, radial_cells, lanes)
        work = [
            scratch(2, 2, 2, rows, lanes),
            scratch(2, 2, 2, rows, lanes),
            scratch(3 * cells, lanes),
            scratch(cells + 2 * (SWEEPS - 1), TILE, lanes),
        ]
        levels = scratch(SWEEPS, 2, 2, SWEEPS, rows, lanes)
        if not known:
            operands += (inner_cut,)
            cut, edge, ends_now, fixed_tiles, beyond = call(
                functools.partial(finish, step),
                (
                    array(1, 2, cells, SWEEPS, lanes),
                    array(cells, lanes),
                    array(*last),
                    tiles,
                    array(2, 2, 2, span, lanes),
                ),
                [smem] + [vmem] * (len(operands) - 1),
                [vmem] * 5,
                [levels, *work],
                operands,
                26,
                name="finish",
            )
            ends = (ends_now, b_ends, w_ends)
        else:
            operands += (beyond,)
            pressure = call(
                functools.partial(finish, step),
                result,
                [smem] + [vmem] * (len(operands) - 1) + [hbm],
                hbm,
                [
                    levels,
                    scratch(*last),
                    scratch(*tiles.shape),
                    *work,
                    pltpu.SemaphoreType.DMA((5,)),
                ],
                (*operands, done),
                26,
                input_output_aliases={len(operands): 0},
                name="finish",
            )
    return pressure


def solution(mesh):
    placed = (
        P(None, "az", "rad", None),
        P(None, "az", "rad", None),
        P(None, "az", "rad", None),
        P(),
    )
    return jax.shard_map(
        per_device,
        mesh=mesh,
        in_specs=placed,
        out_specs=P(None, "az", "rad", None),
        check_vma=False,
    )
```

profile of v0, /device:TPU:1, one launch (start us, length us, event | category | flops | bytes accessed | tf_op | source)
XLA Modules:
  0.0 53.7 jit_solution(2167277896659484078)
XLA Ops:
  0.0 1.8 %pack.1 = (f32[3,2,16,4,128]{4,3,2,1,0:T(4,128)S(1)}, f32[16,128]{1,0:T(8,128)S(1)}, f32[2,2,4,96,128]{4,3,2,1,0:T(8,128)S(1)}, f32[2,2,3,96,128]{4,3,2,1,0:T(8,128)S(1)}, f32[2,2,3,96,128]{4,3,2,1,0:T(8,128)S(1)}) custom-call(f32[2,16,96,128]{3,2,1,0:T(8,128)} %p_ref.3, f32[2,16,96,128]{3,2,1,0:T(8,128)} %s_ref.3, f32[2,16,96,128]{3,2,1,0:T(8,128)} %d_ref.3), custom_call_target="tpu_custom_call" | custom-call | flops 319488 | bytes 212992 | tf_op jit(solution)/shard_map/pack/pallas_call | solution.py:726
  1.8 2.1 %collective-permute-start.32 = (f32[3,2,16,4,128]{4,3,2,1,0:T(4,128)S(1)}, f32[3,2,16,4,128]{4,3,2,1,0:T(4,128)S(1)}, u32[]{:S(2)}, u32[]{:S(2)}) collective-permute-start(f32[3,2,16,4,128]{4,3,2,1,0:T(4,128)S(1)} %get-tuple-element.98), channel_id=1, source_target_pairs={{0,1},{1,0},{2,3},{3,2},{4,5},{5,4},{6,7},{7,6},{8,9},{9,8},{10,11... | collective-permute-start | bytes 589832 | tf_op jit(solution)/shard_map/ppermute | solution.py:762
  4.6 4.3 %conditional.2 = (f32[16,128]{1,0:T(8,128)}) conditional(s32[]{:T(128)} %clamp.6, f32[16,128]{1,0:T(8,128)S(1)} %get-tuple-element.104, f32[16,128]{1,0:T(8,128)S(1)} %get-tuple-element.104, f32[16,128]{1,0:T(8,128)S(1)} %get-tuple-element.104, f32[16,128]{1,0:T(8,128)S(1)} %get-tuple-element.104, ...), branch_computations={%region_0.1_spmd, %region_1.2_spmd, %region_2.3_spmd, %region_3.4_... | conditional | bytes 32816 | solution.py:695
  4.7 2.1 %collective-permute-start.13 = (f32[16,128]{1,0:T(8,128)S(1)}, f32[16,128]{1,0:T(8,128)}, u32[]{:S(2)}, u32[]{:S(2)}) collective-permute-start(f32[16,128]{1,0:T(8,128)S(1)} %param.13), channel_id=1, source_target_pairs={{7,0},{26,1},{9,2},{28,3},{11,4},{30,5},{13,6},{0,7},{15,8},{2,9},... | collective-permute-start | bytes 24584 | tf_op jit(solution)/shard_map/cond/branch_13_fun/ppermute | solution.py:691
  6.8 2.1 %collective-permute-done.13 = f32[16,128]{1,0:T(8,128)} collective-permute-done((f32[16,128]{1,0:T(8,128)S(1)}, f32[16,128]{1,0:T(8,128)}, u32[]{:S(2)}, u32[]{:S(2)}) %collective-permute-start.13) | collective-permute-done | bytes 8224 | tf_op jit(solution)/shard_map/cond/branch_13_fun/ppermute | solution.py:691
  8.9 0.0 collective-permute-done.32.cut_ref
  8.9 1.0 %edges.2 = (f32[1184,128]{1,0:T(8,128)S(1)}, f32[1184,128]{1,0:T(8,128)S(1)}) custom-call(f32[2,2,4,96,128]{4,3,2,1,0:T(8,128)S(1)} %get-tuple-element.106.p_ends, f32[2,2,3,96,128]{4,3,2,1,0:T(8,128)S(1)} %get-tuple-element.107.s_ends, f32[2,2,3,96,128]{4,3,2,1,0:T(8,128)S(1)} %get-tuple-element.108.d_ends, ...), custom_call_target="tpu_custom_call" | custom-call | flops 3833856 | bytes 2555904 | tf_op jit(solution)/shard_map/edges/pallas_call | solution.py:726
  9.9 2.9 %collective-permute-start.33 = (f32[1184,128]{1,0:T(8,128)S(1)}, f32[1184,128]{1,0:T(8,128)S(1)}, u32[]{:S(2)}, u32[]{:S(2)}) collective-permute-start(f32[1184,128]{1,0:T(8,128)S(1)} %get-tuple-element.109), channel_id=1, source_target_pairs={{0,2},{2,4},{4,6},{6,8},{8,10},{10,12},{12,14},{14,16},{16,18},{18... | collective-permute-start | bytes 1818632 | tf_op jit(solution)/shard_map/ppermute | solution.py:777
  12.8 0.0 collective-permute-start.34
  12.8 7.9 %interior.2 = (f32[2,4,2,2,128,128]{5,4,3,2,1,0:T(8,128)S(1)}, f32[8,8,128]{2,1,0:T(8,128)S(1)}, f32[16,8,128]{2,1,0:T(8,128)S(1)}, f32[2,8,4,128]{3,2,1,0:T(4,1...) custom-call(f32[2,16,96,128]{3,2,1,0:T(8,128)} %p_ref.3, ...), custom_call_target="tpu_custom_call" | custom-call | flops 14057472 | bytes 9371648 | tf_op jit(solution)/shard_map/interior/pallas_call | solution.py:726
  20.8 5.5 %collective-permute-done.33.left_ref = f32[1184,128]{1,0:T(8,128)S(1)} collective-permute-done((f32[1184,128]{1,0:T(8,128)S(1)}, f32[1184,128]{1,0:T(8,128)S(1)}, u32[]{:S(2)}, u32[]{:S(2)}) %collective-permute-start.33) | collective-permute-done | bytes 606240 | tf_op jit(solution)/shard_map/ppermute | solution.py:777
  26.3 2.5 %collective-permute-done.34.right_ref = f32[1184,128]{1,0:T(8,128)S(1)} collective-permute-done((f32[1184,128]{1,0:T(8,128)S(1)}, f32[1184,128]{1,0:T(8,128)S(1)}, u32[]{:S(2)}, u32[]{:S(2)}) %collective-permute-start.34) | collective-permute-done | bytes 606240 | tf_op jit(solution)/shard_map/ppermute | solution.py:778
  28.8 2.1 %finish.2 = (f32[1,2,16,4,128]{4,3,2,1,0:T(4,128)S(1)}, f32[16,128]{1,0:T(8,128)S(1)}, f32[2,2,4,96,128]{4,3,2,1,0:T(8,128)S(1)}, f32[8,8,128]{2,1,0:T(8,128)S(1)}, f32[2,2,2,104,128]{4,3,2,1,0:T(8,128)S(1)}) custom-call(s32[1]{0:T(128)} %copy.39.turn_ref, f32[2,2,4,104,128]{4,3,2,1,0:T(8,128)S(1)} %get-tuple-element.99.b_ends, ...), custom_call_target="tpu_custom_call" | custom-call | flops 8306688 | bytes 5537792 | tf_op jit(solution)/shard_map/finish/pallas_call | solution.py:726
  30.9 1.2 %collective-permute-start.35 = (f32[1,2,16,4,128]{4,3,2,1,0:T(4,128)S(1)}, f32[1,2,16,4,128]{4,3,2,1,0:T(4,128)S(1)}, u32[]{:S(2)}, u32[]{:S(2)}) collective-permute-start(f32[1,2,16,4,128]{4,3,2,1,0:T(4,128)S(1)} %get-tuple-element.116), channel_id=1, source_target_pairs={{0,1},{1,0},{2,3},{3,2},{4,5},{5,4},{6,7},{7,6},{8,9},{9,8},{10,11... | collective-permute-start | bytes 196616 | tf_op jit(solution)/shard_map/ppermute | solution.py:762
  32.2 4.4 %conditional.3 = (f32[16,128]{1,0:T(8,128)}) conditional(s32[]{:T(128)} %clamp.7, f32[16,128]{1,0:T(8,128)S(1)} %get-tuple-element.119, f32[16,128]{1,0:T(8,128)S(1)} %get-tuple-element.119, f32[16,128]{1,0:T(8,128)S(1)} %get-tuple-element.119, f32[16,128]{1,0:T(8,128)S(1)} %get-tuple-element.119, ...), branch_computations={%region_16.17_spmd, %region_17.18_spmd, %region_18.19_spmd, %regio... | conditional | bytes 32816 | solution.py:695
  32.2 0.0 collective-permute-start.26
  32.2 4.4 %collective-permute-done.26 = f32[16,128]{1,0:T(8,128)} collective-permute-done((f32[16,128]{1,0:T(8,128)S(1)}, f32[16,128]{1,0:T(8,128)}, u32[]{:S(2)}, u32[]{:S(2)}) %collective-permute-start.26) | collective-permute-done | bytes 8224 | tf_op jit(solution)/shard_map/cond/branch_10_fun/ppermute | solution.py:691
  36.6 1.1 %edges.3 = (f32[792,128]{1,0:T(8,128)S(1)}, f32[792,128]{1,0:T(8,128)S(1)}) custom-call(f32[2,2,4,96,128]{4,3,2,1,0:T(8,128)S(1)} %get-tuple-element.113.p_ends, f32[2,2,4,104,128]{4,3,2,1,0:T(8,128)S(1)} %get-tuple-element.99.b_ends, f32[2,2,4,104,128]{4,3,2,1,0:T(8,128)S(1)} %get-tuple-element.100.w_ends, ...), custom_call_target="tpu_custom_call" | custom-call | flops 3833856 | bytes 2555904 | tf_op jit(solution)/shard_map/edges/pallas_call | solution.py:726
  37.7 2.4 %collective-permute-start.36 = (f32[792,128]{1,0:T(8,128)S(1)}, f32[792,128]{1,0:T(8,128)S(1)}, u32[]{:S(2)}, u32[]{:S(2)}) collective-permute-start(f32[792,128]{1,0:T(8,128)S(1)} %get-tuple-element.121), channel_id=1, source_target_pairs={{0,2},{2,4},{4,6},{6,8},{8,10},{10,12},{12,14},{14,16},{16,18},{18... | collective-permute-start | bytes 1216520 | tf_op jit(solution)/shard_map/ppermute | solution.py:777
  40.1 0.0 collective-permute-start.37
  40.1 7.2 %interior.3 = (f32[2,16,96,128]{3,2,1,0:T(8,128)}, f32[2,4,2,2,128,128]{5,4,3,2,1,0:T(8,128)S(1)}, f32[8,8,128]{2,1,0:T(8,128)S(1)}, f32[16,8,128]{2,1,0:T(8,128)S(1)}) custom-call(f32[2,8,96,128]{3,2,1,0:T(8,128)} %get-tuple-element.101.inner_ref, f32[8,8,128]{2,1,0:T(8,128)S(1)} %get-tuple-element.112.tile_ref, ...), custom_call_target="tpu_custom_call" | custom-call | flops 14057472 | bytes 9371648 | tf_op jit(solution)/shard_map/interior/pallas_call | solution.py:726
  47.3 2.0 %collective-permute-done.36.left_ref = f32[792,128]{1,0:T(8,128)S(1)} collective-permute-done((f32[792,128]{1,0:T(8,128)S(1)}, f32[792,128]{1,0:T(8,128)S(1)}, u32[]{:S(2)}, u32[]{:S(2)}) %collective-permute-start.36) | collective-permute-done | bytes 405536 | tf_op jit(solution)/shard_map/ppermute | solution.py:777
  49.3 1.2 %collective-permute-done.37.right_ref = f32[792,128]{1,0:T(8,128)S(1)} collective-permute-done((f32[792,128]{1,0:T(8,128)S(1)}, f32[792,128]{1,0:T(8,128)S(1)}, u32[]{:S(2)}, u32[]{:S(2)}) %collective-permute-start.37) | collective-permute-done | bytes 405536 | tf_op jit(solution)/shard_map/ppermute | solution.py:778
  50.4 3.1 %finish.3 = f32[2,16,96,128]{3,2,1,0:T(8,128)} custom-call(s32[1]{0:T(128)} %copy.39.turn_ref, f32[2,2,4,104,128]{4,3,2,1,0:T(8,128)S(1)} %get-tuple-element.99.b_ends, f32[2,2,4,104,128]{4,3,2,1,0:T(8,128)S(1)} %get-tuple-element.100.w_ends, f32[16,8,128]{2,1,0:T(8,128)S(1)} %get-tuple-element.117.w_tile, ...), custom_call_target="tpu_custom_call", output_to_operand_aliasing={{}: (10, {})} | custom-call | flops 8306688 | bytes 5537792 | tf_op jit(solution)/shard_map/finish/pallas_call | solution.py:726
  (1 shorter events, 0.0 us)
Async XLA Ops:
  1.8 7.1 %collective-permute-start.32 = (f32[3,2,16,4,128]{4,3,2,1,0:T(4,128)S(1)}, f32[3,2,16,4,128]{4,3,2,1,0:T(4,128)S(1)}, u32[]{:S(2)}, u32[]{:S(2)}) collective-permute-start(f32[3,2,16,4,128]{4,3,2,1,0:T(4,128)S(1)} %get-tuple-element.98), channel_id=1, source_target_pairs={{0,1},{1,0},{2,3},{3,2},{4,5},{5,4},{6,7},{7,6},{8,9},{9,8},{10,11... | collective-permute-start | bytes 589832 | tf_op jit(solution)/shard_map/ppermute | solution.py:762
  4.7 4.3 %collective-permute-start.13 = (f32[16,128]{1,0:T(8,128)S(1)}, f32[16,128]{1,0:T(8,128)}, u32[]{:S(2)}, u32[]{:S(2)}) collective-permute-start(f32[16,128]{1,0:T(8,128)S(1)} %param.13), channel_id=1, source_target_pairs={{7,0},{26,1},{9,2},{28,3},{11,4},{30,5},{13,6},{0,7},{15,8},{2,9},... | collective-permute-start | bytes 24584 | tf_op jit(solution)/shard_map/cond/branch_13_fun/ppermute | solution.py:691
  9.9 16.4 %collective-permute-start.33 = (f32[1184,128]{1,0:T(8,128)S(1)}, f32[1184,128]{1,0:T(8,128)S(1)}, u32[]{:S(2)}, u32[]{:S(2)}) collective-permute-start(f32[1184,128]{1,0:T(8,128)S(1)} %get-tuple-element.109), channel_id=1, source_target_pairs={{0,2},{2,4},{4,6},{6,8},{8,10},{10,12},{12,14},{14,16},{16,18},{18... | collective-permute-start | bytes 1818632 | tf_op jit(solution)/shard_map/ppermute | solution.py:777
  12.8 16.0 %collective-permute-start.34 = (f32[1184,128]{1,0:T(8,128)S(1)}, f32[1184,128]{1,0:T(8,128)S(1)}, u32[]{:S(2)}, u32[]{:S(2)}) collective-permute-start(f32[1184,128]{1,0:T(8,128)S(1)} %get-tuple-element.110), channel_id=1, source_target_pairs={{0,30},{2,0},{4,2},{6,4},{8,6},{10,8},{12,10},{14,12},{16,14},{18,... | collective-permute-start | bytes 1818632 | tf_op jit(solution)/shard_map/ppermute | solution.py:778
  30.9 5.6 %collective-permute-start.35 = (f32[1,2,16,4,128]{4,3,2,1,0:T(4,128)S(1)}, f32[1,2,16,4,128]{4,3,2,1,0:T(4,128)S(1)}, u32[]{:S(2)}, u32[]{:S(2)}) collective-permute-start(f32[1,2,16,4,128]{4,3,2,1,0:T(4,128)S(1)} %get-tuple-element.116), channel_id=1, source_target_pairs={{0,1},{1,0},{2,3},{3,2},{4,5},{5,4},{6,7},{7,6},{8,9},{9,8},{10,11... | collective-permute-start | bytes 196616 | tf_op jit(solution)/shard_map/ppermute | solution.py:762
  32.2 4.4 %collective-permute-start.26 = (f32[16,128]{1,0:T(8,128)S(1)}, f32[16,128]{1,0:T(8,128)}, u32[]{:S(2)}, u32[]{:S(2)}) collective-permute-start(f32[16,128]{1,0:T(8,128)S(1)} %param.26), channel_id=1, source_target_pairs={{13,0},{20,1},{15,2},{22,3},{17,4},{24,5},{19,6},{26,7},{21,8},{28... | collective-permute-start | bytes 24584 | tf_op jit(solution)/shard_map/cond/branch_10_fun/ppermute | solution.py:691
  37.7 11.6 %collective-permute-start.36 = (f32[792,128]{1,0:T(8,128)S(1)}, f32[792,128]{1,0:T(8,128)S(1)}, u32[]{:S(2)}, u32[]{:S(2)}) collective-permute-start(f32[792,128]{1,0:T(8,128)S(1)} %get-tuple-element.121), channel_id=1, source_target_pairs={{0,2},{2,4},{4,6},{6,8},{8,10},{10,12},{12,14},{14,16},{16,18},{18... | collective-permute-start | bytes 1216520 | tf_op jit(solution)/shard_map/ppermute | solution.py:777
  40.1 10.4 %collective-permute-start.37 = (f32[792,128]{1,0:T(8,128)S(1)}, f32[792,128]{1,0:T(8,128)S(1)}, u32[]{:S(2)}, u32[]{:S(2)}) collective-permute-start(f32[792,128]{1,0:T(8,128)S(1)} %get-tuple-element.122), channel_id=1, source_target_pairs={{0,30},{2,0},{4,2},{6,4},{8,6},{10,8},{12,10},{14,12},{16,14},{18,... | collective-permute-start | bytes 1216520 | tf_op jit(solution)/shard_map/ppermute | solution.py:778
where the time goes:
time: 53.4 us; the launch traced here: 53.7 us
  Pallas kernels  24.3 us (46%)
  waiting for transfers between devices  17.7 us (33%)
  starting transfers between devices  10.8 us (20%)
  between operations  0.94 us (2%)
    pallas_call x7, Pallas kernels, call(): pl.pallas_call(kernel, out_shape=out_shape, in_specs=in_specs, out_specs=...  24.3 us
    ppermute x2, waiting for transfers between devices, per_device(): left = lax.ppermute(last, 'az', ring(size, 1))  7.53 us
    ppermute x2, waiting for transfers between devices, branch(): return lambda e: lax.ppermute(e, ('az', 'rad'), facing_pairs(size, t))  6.51 us
    ppermute x2, starting transfers between devices, per_device(): left = lax.ppermute(last, 'az', ring(size, 1))  5.28 us
    ppermute x2, waiting for transfers between devices, per_device(): right = lax.ppermute(first, 'az', ring(size, -1))  3.67 us
    ppermute x2, starting transfers between devices, per_device(): cut = lax.ppermute(cut, 'rad', [(0, 1), (1, 0)])  3.36 us
    ppermute x2, starting transfers between devices, branch(): return lambda e: lax.ppermute(e, ('az', 'rad'), facing_pairs(size, t))  2.15 us
  transfers between devices with their start and end apart: 8, of which 6 were waited for; matrix products, arithmetic and copies ran while one was open for 0% of the time, Pallas kernels for 28%

commit v1 on v0

--- a/solution.py
+++ b/solution.py
@@ -467,7 +467,7 @@
     on_each_side(radial_cells, body)
 
 
-def ghost_response(side, step, turn_ref, w_tile, block_ref, layout, messages, weights, wide, source):
+def ghost_response(side, step, turn_ref, w_tile, block_ref, layout, messages, weights, wide, source, matrix):
     facing = side.facing
     cells = w_tile.shape[0]
     reach = SWEEPS - 1
@@ -499,12 +499,14 @@
     for n in range(1, SWEEPS):
         old = response
         response = list(old)
+        axial = axial_product(jnp.concatenate(old, axis=0), matrix)
         for c in range(n, len(old) - n):
             x = old[c]
             radial = jnp.where(row == 0, 0.0, pltpu.roll(x, 1, 0)) + jnp.where(
                 row == TILE - 1, 0.0, pltpu.roll(x, TILE - 1, 0)
             )
-            nbr = (old[c - 1] + old[c + 1]) + (radial + axial_sum(x)) + given[c]
+            along = axial[c * TILE : (c + 1) * TILE]
+            nbr = (old[c - 1] + old[c + 1]) + (radial + along) + given[c]
             response[c] = (1.0 - OMEGA) * x + weight[c] * nbr
     return response[reach : reach + cells]
 
@@ -622,7 +624,7 @@
         for k in (1 - facing, facing):
             if k == facing:
                 response = ghost_response(
-                    side, step, turn_ref, w_tile, block_ref, layout, messages, weights, wide, source
+                    side, step, turn_ref, w_tile, block_ref, layout, messages, weights, wide, source, matrix
                 )
                 for i in range(cells - 2 * SWEEPS):
                     inner_tiles[i] = tile_in[i] + response[SWEEPS + i]

time: 53.4 us -> 53.5 us (level); the launches traced: 53.7 us -> 53 us
  starting transfers between devices: 10.8 us -> 9.23 us
  Pallas kernels: 24.3 us -> 24.9 us
    ppermute x2, waiting for transfers between devices: 3.67 us -> 4.96 us  [per_device(): right = lax.ppermute(first, 'az', ring(size, -1))]
    ppermute x2, waiting for transfers between devices: 6.51 us -> 5.44 us  [branch(): return lambda e: lax.ppermute(e, ('az', 'rad'), facing_pairs(size, t))]
    ppermute x2, starting transfers between devices: 5.28 us -> 4.38 us  [per_device(): left = lax.ppermute(last, 'az', ring(size, 1))]
    ppermute x2, starting transfers between devices: 3.36 us -> 2.52 us  [per_device(): cut = lax.ppermute(cut, 'rad', [(0, 1), (1, 0)])]
    pallas_call x7, Pallas kernels: 24.3 us -> 24.9 us  [call(): pl.pallas_call(kernel, out_shape=out_shape, in_specs=in_specs, out_specs=...]
  transfers between devices with their start and end apart: 8 -> 8, of which waited for: 6 -> 6; matrix products, arithmetic and copies ran while one was open for 0% -> 0% of each run, Pallas kernels for 28% -> 29%
where the time goes in v1:
time: 53.5 us; the launch traced here: 53 us
  Pallas kernels  24.9 us (47%)
  waiting for transfers between devices  17.9 us (33%)
  starting transfers between devices  9.23 us (17%)
  between operations  0.93 us (2%)
    pallas_call x7, Pallas kernels, call(): pl.pallas_call(kernel, out_shape=out_shape, in_specs=in_specs, out_specs=...  24.9 us
    ppermute x2, waiting for transfers between devices, per_device(): left = lax.ppermute(last, 'az', ring(size, 1))  7.52 us
    ppermute x2, waiting for transfers between devices, branch(): return lambda e: lax.ppermute(e, ('az', 'rad'), facing_pairs(size, t))  5.44 us
    ppermute x2, waiting for transfers between devices, per_device(): right = lax.ppermute(first, 'az', ring(size, -1))  4.96 us
    ppermute x2, starting transfers between devices, per_device(): left = lax.ppermute(last, 'az', ring(size, 1))  4.38 us
    ppermute x2, starting transfers between devices, per_device(): cut = lax.ppermute(cut, 'rad', [(0, 1), (1, 0)])  2.52 us
    ppermute x2, starting transfers between devices, branch(): return lambda e: lax.ppermute(e, ('az', 'rad'), facing_pairs(size, t))  2.32 us
  transfers between devices with their start and end apart: 8, of which 6 were waited for; matrix products, arithmetic and copies ran while one was open for 0% of the time, Pallas kernels for 29%

profile of v1, /device:TPU:1, one launch (start us, length us, event | category | flops | bytes accessed | tf_op | source)
XLA Modules:
  0.0 53.0 jit_solution(13473603888236489394)
XLA Ops:
  0.0 1.8 %pack.1 = (f32[3,2,16,4,128]{4,3,2,1,0:T(4,128)S(1)}, f32[16,128]{1,0:T(8,128)S(1)}, f32[2,2,4,96,128]{4,3,2,1,0:T(8,128)S(1)}, f32[2,2,3,96,128]{4,3,2,1,0:T(8,128)S(1)}, f32[2,2,3,96,128]{4,3,2,1,0:T(8,128)S(1)}) custom-call(f32[2,16,96,128]{3,2,1,0:T(8,128)} %p_ref.3, f32[2,16,96,128]{3,2,1,0:T(8,128)} %s_ref.3, f32[2,16,96,128]{3,2,1,0:T(8,128)} %d_ref.3), custom_call_target="tpu_custom_call" | custom-call | flops 319488 | bytes 212992 | tf_op jit(solution)/shard_map/pack/pallas_call | solution.py:728
  1.8 2.1 %collective-permute-start.32 = (f32[3,2,16,4,128]{4,3,2,1,0:T(4,128)S(1)}, f32[3,2,16,4,128]{4,3,2,1,0:T(4,128)S(1)}, u32[]{:S(2)}, u32[]{:S(2)}) collective-permute-start(f32[3,2,16,4,128]{4,3,2,1,0:T(4,128)S(1)} %get-tuple-element.98), channel_id=1, source_target_pairs={{0,1},{1,0},{2,3},{3,2},{4,5},{5,4},{6,7},{7,6},{8,9},{9,8},{10,11... | collective-permute-start | bytes 589832 | tf_op jit(solution)/shard_map/ppermute | solution.py:764
  4.6 4.6 %conditional.2 = (f32[16,128]{1,0:T(8,128)}) conditional(s32[]{:T(128)} %clamp.6, f32[16,128]{1,0:T(8,128)S(1)} %get-tuple-element.104, f32[16,128]{1,0:T(8,128)S(1)} %get-tuple-element.104, f32[16,128]{1,0:T(8,128)S(1)} %get-tuple-element.104, f32[16,128]{1,0:T(8,128)S(1)} %get-tuple-element.104, ...), branch_computations={%region_0.1_spmd, %region_1.2_spmd, %region_2.3_spmd, %region_3.4_... | conditional | bytes 32816 | solution.py:697
  4.7 2.3 %collective-permute-start.8 = (f32[16,128]{1,0:T(8,128)S(1)}, f32[16,128]{1,0:T(8,128)}, u32[]{:S(2)}, u32[]{:S(2)}) collective-permute-start(f32[16,128]{1,0:T(8,128)S(1)} %param.8), channel_id=1, source_target_pairs={{17,0},{16,1},{19,2},{18,3},{21,4},{20,5},{23,6},{22,7},{25,8},{24... | collective-permute-start | bytes 24584 | tf_op jit(solution)/shard_map/cond/branch_8_fun/ppermute | solution.py:693
  7.0 2.3 %collective-permute-done.8 = f32[16,128]{1,0:T(8,128)} collective-permute-done((f32[16,128]{1,0:T(8,128)S(1)}, f32[16,128]{1,0:T(8,128)}, u32[]{:S(2)}, u32[]{:S(2)}) %collective-permute-start.8) | collective-permute-done | bytes 8224 | tf_op jit(solution)/shard_map/cond/branch_8_fun/ppermute | solution.py:693
  9.2 0.0 collective-permute-done.32.cut_ref
  9.2 1.0 %edges.2 = (f32[1184,128]{1,0:T(8,128)S(1)}, f32[1184,128]{1,0:T(8,128)S(1)}) custom-call(f32[2,2,4,96,128]{4,3,2,1,0:T(8,128)S(1)} %get-tuple-element.106.p_ends, f32[2,2,3,96,128]{4,3,2,1,0:T(8,128)S(1)} %get-tuple-element.107.s_ends, f32[2,2,3,96,128]{4,3,2,1,0:T(8,128)S(1)} %get-tuple-element.108.d_ends, ...), custom_call_target="tpu_custom_call" | custom-call | flops 3833856 | bytes 2555904 | tf_op jit(solution)/shard_map/edges/pallas_call | solution.py:728
  10.2 3.1 %collective-permute-start.33 = (f32[1184,128]{1,0:T(8,128)S(1)}, f32[1184,128]{1,0:T(8,128)S(1)}, u32[]{:S(2)}, u32[]{:S(2)}) collective-permute-start(f32[1184,128]{1,0:T(8,128)S(1)} %get-tuple-element.109), channel_id=1, source_target_pairs={{0,2},{2,4},{4,6},{6,8},{8,10},{10,12},{12,14},{14,16},{16,18},{18... | collective-permute-start | bytes 1818632 | tf_op jit(solution)/shard_map/ppermute | solution.py:779
  13.4 0.0 collective-permute-start.34
  13.4 7.9 %interior.2 = (f32[2,4,2,2,128,128]{5,4,3,2,1,0:T(8,128)S(1)}, f32[8,8,128]{2,1,0:T(8,128)S(1)}, f32[16,8,128]{2,1,0:T(8,128)S(1)}, f32[2,8,4,128]{3,2,1,0:T(4,1...) custom-call(f32[2,16,96,128]{3,2,1,0:T(8,128)} %p_ref.3, ...), custom_call_target="tpu_custom_call" | custom-call | flops 14057472 | bytes 9371648 | tf_op jit(solution)/shard_map/interior/pallas_call | solution.py:728
  21.3 5.5 %collective-permute-done.33.left_ref = f32[1184,128]{1,0:T(8,128)S(1)} collective-permute-done((f32[1184,128]{1,0:T(8,128)S(1)}, f32[1184,128]{1,0:T(8,128)S(1)}, u32[]{:S(2)}, u32[]{:S(2)}) %collective-permute-start.33) | collective-permute-done | bytes 606240 | tf_op jit(solution)/shard_map/ppermute | solution.py:779
  26.9 2.5 %collective-permute-done.34.right_ref = f32[1184,128]{1,0:T(8,128)S(1)} collective-permute-done((f32[1184,128]{1,0:T(8,128)S(1)}, f32[1184,128]{1,0:T(8,128)S(1)}, u32[]{:S(2)}, u32[]{:S(2)}) %collective-permute-start.34) | collective-permute-done | bytes 606240 | tf_op jit(solution)/shard_map/ppermute | solution.py:780
  29.4 2.5 %finish.2 = (f32[1,2,16,4,128]{4,3,2,1,0:T(4,128)S(1)}, f32[16,128]{1,0:T(8,128)S(1)}, f32[2,2,4,96,128]{4,3,2,1,0:T(8,128)S(1)}, f32[8,8,128]{2,1,0:T(8,128)S(1)}, f32[2,2,2,104,128]{4,3,2,1,0:T(8,128)S(1)}) custom-call(s32[1]{0:T(128)} %copy.39.turn_ref, f32[2,2,4,104,128]{4,3,2,1,0:T(8,128)S(1)} %get-tuple-element.99.b_ends, ...), custom_call_target="tpu_custom_call" | custom-call | flops 8306688 | bytes 5537792 | tf_op jit(solution)/shard_map/finish/pallas_call | solution.py:728
  31.8 0.4 collective-permute-start.35
  32.2 3.2 %conditional.3 = (f32[16,128]{1,0:T(8,128)}) conditional(s32[]{:T(128)} %clamp.7, f32[16,128]{1,0:T(8,128)S(1)} %get-tuple-element.119, f32[16,128]{1,0:T(8,128)S(1)} %get-tuple-element.119, f32[16,128]{1,0:T(8,128)S(1)} %get-tuple-element.119, f32[16,128]{1,0:T(8,128)S(1)} %get-tuple-element.119, ...), branch_computations={%region_16.17_spmd, %region_17.18_spmd, %region_18.19_spmd, %regio... | conditional | bytes 32816 | solution.py:697
  32.2 3.2 %collective-permute-done.17 = f32[16,128]{1,0:T(8,128)} collective-permute-done((f32[16,128]{1,0:T(8,128)S(1)}, f32[16,128]{1,0:T(8,128)}, u32[]{:S(2)}, u32[]{:S(2)}) %collective-permute-start.17) | collective-permute-done | bytes 8224 | tf_op jit(solution)/shard_map/cond/branch_1_fun/ppermute | solution.py:693
  35.4 0.0 collective-permute-done.35.cut_ref
  35.4 1.1 %edges.3 = (f32[792,128]{1,0:T(8,128)S(1)}, f32[792,128]{1,0:T(8,128)S(1)}) custom-call(f32[2,2,4,96,128]{4,3,2,1,0:T(8,128)S(1)} %get-tuple-element.113.p_ends, f32[2,2,4,104,128]{4,3,2,1,0:T(8,128)S(1)} %get-tuple-element.99.b_ends, f32[2,2,4,104,128]{4,3,2,1,0:T(8,128)S(1)} %get-tuple-element.100.w_ends, ...), custom_call_target="tpu_custom_call" | custom-call | flops 3833856 | bytes 2555904 | tf_op jit(solution)/shard_map/edges/pallas_call | solution.py:728
  36.5 1.2 %collective-permute-start.36 = (f32[792,128]{1,0:T(8,128)S(1)}, f32[792,128]{1,0:T(8,128)S(1)}, u32[]{:S(2)}, u32[]{:S(2)}) collective-permute-start(f32[792,128]{1,0:T(8,128)S(1)} %get-tuple-element.121), channel_id=1, source_target_pairs={{0,2},{2,4},{4,6},{6,8},{8,10},{10,12},{12,14},{14,16},{16,18},{18... | collective-permute-start | bytes 1216520 | tf_op jit(solution)/shard_map/ppermute | solution.py:779
  37.7 0.0 collective-permute-start.37
  37.7 7.2 %interior.3 = (f32[2,16,96,128]{3,2,1,0:T(8,128)}, f32[2,4,2,2,128,128]{5,4,3,2,1,0:T(8,128)S(1)}, f32[8,8,128]{2,1,0:T(8,128)S(1)}, f32[16,8,128]{2,1,0:T(8,128)S(1)}) custom-call(f32[2,8,96,128]{3,2,1,0:T(8,128)} %get-tuple-element.101.inner_ref, f32[8,8,128]{2,1,0:T(8,128)S(1)} %get-tuple-element.112.tile_ref, ...), custom_call_target="tpu_custom_call" | custom-call | flops 14057472 | bytes 9371648 | tf_op jit(solution)/shard_map/interior/pallas_call | solution.py:728
  44.9 2.0 %collective-permute-done.36.left_ref = f32[792,128]{1,0:T(8,128)S(1)} collective-permute-done((f32[792,128]{1,0:T(8,128)S(1)}, f32[792,128]{1,0:T(8,128)S(1)}, u32[]{:S(2)}, u32[]{:S(2)}) %collective-permute-start.36) | collective-permute-done | bytes 405536 | tf_op jit(solution)/shard_map/ppermute | solution.py:779
  46.9 2.5 %collective-permute-done.37.right_ref = f32[792,128]{1,0:T(8,128)S(1)} collective-permute-done((f32[792,128]{1,0:T(8,128)S(1)}, f32[792,128]{1,0:T(8,128)S(1)}, u32[]{:S(2)}, u32[]{:S(2)}) %collective-permute-start.37) | collective-permute-done | bytes 405536 | tf_op jit(solution)/shard_map/ppermute | solution.py:780
  49.4 3.5 %finish.3 = f32[2,16,96,128]{3,2,1,0:T(8,128)} custom-call(s32[1]{0:T(128)} %copy.39.turn_ref, f32[2,2,4,104,128]{4,3,2,1,0:T(8,128)S(1)} %get-tuple-element.99.b_ends, f32[2,2,4,104,128]{4,3,2,1,0:T(8,128)S(1)} %get-tuple-element.100.w_ends, f32[16,8,128]{2,1,0:T(8,128)S(1)} %get-tuple-element.117.w_tile, ...), custom_call_target="tpu_custom_call", output_to_operand_aliasing={{}: (10, {})} | custom-call | flops 8306688 | bytes 5537792 | tf_op jit(solution)/shard_map/finish/pallas_call | solution.py:728
  (1 shorter events, 0.0 us)
Async XLA Ops:
  1.8 7.5 %collective-permute-start.32 = (f32[3,2,16,4,128]{4,3,2,1,0:T(4,128)S(1)}, f32[3,2,16,4,128]{4,3,2,1,0:T(4,128)S(1)}, u32[]{:S(2)}, u32[]{:S(2)}) collective-permute-start(f32[3,2,16,4,128]{4,3,2,1,0:T(4,128)S(1)} %get-tuple-element.98), channel_id=1, source_target_pairs={{0,1},{1,0},{2,3},{3,2},{4,5},{5,4},{6,7},{7,6},{8,9},{9,8},{10,11... | collective-permute-start | bytes 589832 | tf_op jit(solution)/shard_map/ppermute | solution.py:764
  4.7 4.6 %collective-permute-start.8 = (f32[16,128]{1,0:T(8,128)S(1)}, f32[16,128]{1,0:T(8,128)}, u32[]{:S(2)}, u32[]{:S(2)}) collective-permute-start(f32[16,128]{1,0:T(8,128)S(1)} %param.8), channel_id=1, source_target_pairs={{17,0},{16,1},{19,2},{18,3},{21,4},{20,5},{23,6},{22,7},{25,8},{24... | collective-permute-start | bytes 24584 | tf_op jit(solution)/shard_map/cond/branch_8_fun/ppermute | solution.py:693
  10.2 16.6 %collective-permute-start.33 = (f32[1184,128]{1,0:T(8,128)S(1)}, f32[1184,128]{1,0:T(8,128)S(1)}, u32[]{:S(2)}, u32[]{:S(2)}) collective-permute-start(f32[1184,128]{1,0:T(8,128)S(1)} %get-tuple-element.109), channel_id=1, source_target_pairs={{0,2},{2,4},{4,6},{6,8},{8,10},{10,12},{12,14},{14,16},{16,18},{18... | collective-permute-start | bytes 1818632 | tf_op jit(solution)/shard_map/ppermute | solution.py:779
  13.4 16.0 %collective-permute-start.34 = (f32[1184,128]{1,0:T(8,128)S(1)}, f32[1184,128]{1,0:T(8,128)S(1)}, u32[]{:S(2)}, u32[]{:S(2)}) collective-permute-start(f32[1184,128]{1,0:T(8,128)S(1)} %get-tuple-element.110), channel_id=1, source_target_pairs={{0,30},{2,0},{4,2},{6,4},{8,6},{10,8},{12,10},{14,12},{16,14},{18,... | collective-permute-start | bytes 1818632 | tf_op jit(solution)/shard_map/ppermute | solution.py:780
  31.8 3.6 %collective-permute-start.35 = (f32[1,2,16,4,128]{4,3,2,1,0:T(4,128)S(1)}, f32[1,2,16,4,128]{4,3,2,1,0:T(4,128)S(1)}, u32[]{:S(2)}, u32[]{:S(2)}) collective-permute-start(f32[1,2,16,4,128]{4,3,2,1,0:T(4,128)S(1)} %get-tuple-element.116), channel_id=1, source_target_pairs={{0,1},{1,0},{2,3},{3,2},{4,5},{5,4},{6,7},{7,6},{8,9},{9,8},{10,11... | collective-permute-start | bytes 196616 | tf_op jit(solution)/shard_map/ppermute | solution.py:764
  32.2 3.2 %collective-permute-start.17 = (f32[16,128]{1,0:T(8,128)S(1)}, f32[16,128]{1,0:T(8,128)}, u32[]{:S(2)}, u32[]{:S(2)}) collective-permute-start(f32[16,128]{1,0:T(8,128)S(1)} %param.17), channel_id=1, source_target_pairs={{31,0},{2,1},{1,2},{4,3},{3,4},{6,5},{5,6},{8,7},{7,8},{10,9},{9,1... | collective-permute-start | bytes 24584 | tf_op jit(solution)/shard_map/cond/branch_1_fun/ppermute | solution.py:693
  36.5 10.4 %collective-permute-start.36 = (f32[792,128]{1,0:T(8,128)S(1)}, f32[792,128]{1,0:T(8,128)S(1)}, u32[]{:S(2)}, u32[]{:S(2)}) collective-permute-start(f32[792,128]{1,0:T(8,128)S(1)} %get-tuple-element.121), channel_id=1, source_target_pairs={{0,2},{2,4},{4,6},{6,8},{8,10},{10,12},{12,14},{14,16},{16,18},{18... | collective-permute-start | bytes 1216520 | tf_op jit(solution)/shard_map/ppermute | solution.py:779
  37.7 11.7 %collective-permute-start.37 = (f32[792,128]{1,0:T(8,128)S(1)}, f32[792,128]{1,0:T(8,128)S(1)}, u32[]{:S(2)}, u32[]{:S(2)}) collective-permute-start(f32[792,128]{1,0:T(8,128)S(1)} %get-tuple-element.122), channel_id=1, source_target_pairs={{0,30},{2,0},{4,2},{6,4},{8,6},{10,8},{12,10},{14,12},{16,14},{18,... | collective-permute-start | bytes 1216520 | tf_op jit(solution)/shard_map/ppermute | solution.py:780
